TPU v7x, 32 devices: a whole 2x2x4 slice. The times are simulated.
32 devices in a mesh: maps: 2 (over y), row: 4 (over x, core), col: 4 (over z).
Axes of the slice: x: 2, y: 2, z: 4, core: 2. Of those that a mesh axis runs over, the one named last changes fastest.
Arguments:
- positions: float32 [512, 2, 384], P(('maps', 'row', 'col')), parts along dimension 0, may hold values from 0 to 127
- destination: int32 [512, 1], P(('maps', 'row', 'col')), parts along dimension 0, may hold values from 0 to 15; in each aligned block of 16 rows (0 to 15, 16 to 31, ...) at most 4 rows name the same one
- profile: float32 [65, 65], replicated, may hold values from 0.03 to 1
Outputs:
- magnification: float32 [1024, 512], P(('maps', 'row'), 'col'), parts along dimension 0
There are 2 independent parts, one for each index of `maps`. A program takes and returns all parts, laid end to end along the dimension named above; an argument that names none is the same for every part. Nothing has to cross between parts.
Inputs may be any that keep to these rules, and one draw needn't show every extreme that they name: `destination`: at most 4 of the blocks of one device name one tile.
All inputs are finite; a program needn't handle non-finite values.
Results may differ from a plain program's by a relative error of at most 0.0003.
Values may be sent and summed in bfloat16 or wider, within the bound.
No kernel may reach another device: no remote copies, remote signals or barrier semaphores. Data moves between devices by JAX's collectives and lax.ppermute only.
A program may use at most 64 MiB of HBM per device.

v0:
```python
import functools

import jax
import jax.numpy as jnp
from jax import lax
from jax.experimental import pallas as pl
from jax.experimental.pallas import tpu as pltpu
from jax.sharding import PartitionSpec as P

TILE = 128
HALO = 32
MOST = 4
DISC = 2 * HALO + 1
STEP = 16
LONG = TILE + STEP
TURNS = 2 * HALO // STEP
WIDE = TILE + 2 * HALO
LANES = 128
SPAN = 64
BATCH = 8
ROOM = 5
COMMON = 3
COUNT = 16
KINDS = 18
FAR = 1024.0

VMEM = pl.BlockSpec(memory_space=pltpu.VMEM)
SMEM = pl.BlockSpec(memory_space=pltpu.SMEM)
ALONE = pltpu.CompilerParams(vmem_limit_bytes=67_104_000)
LIMIT = pltpu.CompilerParams(vmem_limit_bytes=32 * 1024 * 1024)


def touches(distance, least, most):
    before = (distance == -1.0) & (most > TILE - HALO - 1.0)
    after = (distance == 1.0) & (least < HALO)
    return (distance == 0.0) | before | after


def split(index, size):
    index = index.astype(jnp.float32)
    quotient = jnp.floor((index + 0.5) * (1.0 / size))
    return quotient, index - size * quotient


def pack_kernel(turn_ref, dest_ref, rays_ref, out_ref, labels, parts):
    blocks, _, rays = rays_ref.shape
    tiles = out_ref.shape[0] // 8
    width = parts.shape[0]
    col_count = lax.axis_size("col")
    skip = 0.0 if turn_ref is None else 2.0 * ROOM * turn_ref[0].astype(jnp.float32)
    copy, own = split(lax.broadcasted_iota(jnp.int32, (blocks, width), 1), blocks)
    place = lax.broadcasted_iota(jnp.int32, (blocks, width), 0).astype(jnp.float32)
    there = (own == place) & (copy < 3.0)

    def laid(column):
        return jnp.sum(jnp.where(there, column, 0.0), axis=0, keepdims=True)

    labels[...] = jnp.full(labels.shape, -1.0, jnp.float32)
    for g in range(3):
        labels[0:1, g * blocks : (g + 1) * blocks] = dest_ref[...].astype(jnp.float32)
    label = labels[...]
    label_row = jnp.floor((label + 0.5) * (1.0 / col_count))
    label_col = label - label_row * col_count
    first, second = rays_ref[:, 0, :], rays_ref[:, 1, :]
    least_row, most_row = laid(jnp.min(first, 1, keepdims=True)), laid(jnp.max(first, 1, keepdims=True))
    least_col, most_col = laid(jnp.min(second, 1, keepdims=True)), laid(jnp.max(second, 1, keepdims=True))
    earlier = lax.broadcasted_iota(jnp.int32, (width, width), 0).astype(jnp.float32)
    copy, own = split(lax.broadcasted_iota(jnp.int32, (width, width), 1), blocks)
    earlier = jnp.where((earlier < own) & (copy < 3.0), 1.0, 0.0).astype(jnp.bfloat16)

    def chosen(row, col):
        odd = split(row, 2)[1]
        row = row - odd
        dc = label_col - col
        aside = touches(dc, least_col, most_col) & (label >= 0.0)

        def coded(dr):
            reach = aside & touches(dr, least_row, most_row)
            return reach, jnp.where(reach, 3.0 * dr + dc + 4.0, FAR)

        even, odds = coded(label_row - row), coded(label_row - row - 1.0)
        reach = jnp.where(even[0] | odds[0], 1.0, 0.0)
        rank = jnp.dot(reach.astype(jnp.bfloat16), earlier, preferred_element_type=jnp.float32)
        left = rank - skip - odd
        slot = jnp.floor(left * 0.5)
        mine = (reach > 0.0) & (slot * 2.0 == left) & (slot >= 0.0) & (slot < ROOM)
        return jnp.where(mine, slot, -1.0), even[1], odds[1], (rank + 1.0) * reach

    tile = lax.broadcasted_iota(jnp.int32, (tiles, width), 0)
    slot, even, odds, most = chosen(*split(tile, col_count))
    most = jnp.max(jnp.max(most, axis=1, keepdims=True), axis=0, keepdims=True)
    turns = jnp.floor((most + (2.0 * ROOM - 0.5)) / (2.0 * ROOM))
    lane = lax.broadcasted_iota(jnp.int32, (tiles, width), 1)
    meta = jnp.where(lane == COUNT, turns, FAR)
    for k in range(ROOM):
        here = (slot == k) & (lane < blocks)
        for at, code in ((k, even), (8 + k, odds)):
            found = jnp.sum(jnp.where(here, code - FAR, 0.0), axis=1, keepdims=True) + FAR
            meta = jnp.where(lane == at, found, meta)
    for at, code in ((KINDS, even), (KINDS + 1, odds)):
        rowwise, colwise = split(code, 3)
        kind = jnp.where(rowwise == 1.0, 0.0, 2.0) + jnp.where(colwise == 1.0, 0.0, 1.0)
        bit = 1 << jnp.clip(5.0 * kind + slot, 0.0, 23.0).astype(jnp.int32)
        here = (slot >= 0.0) & (code < FAR) & (lane < blocks)
        word = jnp.sum(jnp.where(here, bit.astype(jnp.float32), 0.0), axis=1, keepdims=True)
        meta = jnp.where(lane == at, word, meta)

    parts[...] = jnp.zeros(parts.shape, jnp.float32)
    parts[:blocks, :rays] = first
    parts[:blocks, rays:] = second[:, :LANES]
    parts[blocks : 2 * blocks, : 2 * LANES] = second[:, LANES:]
    parts[2 * blocks : 3 * blocks, 2 * LANES :] = second[:, LANES:]
    parts[3 * blocks : 3 * blocks + tiles, 2 * LANES : 3 * LANES] = meta[:, :LANES]

    tile, within = split(lax.broadcasted_iota(jnp.int32, (8 * tiles, width), 0), 8)
    lane = lax.broadcasted_iota(jnp.int32, (8 * tiles, width), 1)
    copy = split(lane, blocks)[0]
    slot = chosen(*split(tile, col_count))[0]
    low = 2.0 * (within - ROOM)
    wanted = jnp.where(copy == 0.0, within, jnp.where(copy == 1.0, low, low + 1.0))
    place = ((copy == 0.0) & (within < ROOM)) | ((copy > 0.0) & (copy < 3.0) & (within >= ROOM))
    codes = (lane.astype(jnp.float32) - 3.0 * blocks == tile) & (within == 7.0)
    select = jnp.where((place & (slot == wanted)) | codes, 1.0, 0.0).astype(jnp.bfloat16)
    rest = parts[...]
    total = jnp.zeros(out_ref.shape, jnp.float32)
    for _ in range(3):
        part = rest.astype(jnp.bfloat16)
        rest = rest - part.astype(jnp.float32)
        total = total + jnp.dot(select, part, preferred_element_type=jnp.float32)
    out_ref[...] = total


def table_kernel(profile_ref, dest_ref, rays_ref, pairs_ref, last_ref, dest_copy, rays_copy):
    dest_copy[...] = dest_ref[...]
    rays_copy[...] = rays_ref[...]
    a = lax.broadcasted_iota(jnp.int32, (DISC, DISC), 0) - HALO
    c = lax.broadcasted_iota(jnp.int32, (DISC, DISC), 1) - HALO
    weights = jnp.where(a * a + c * c <= HALO * HALO, profile_ref[...], 0.0)
    kernel = (weights / jnp.sum(weights)).astype(jnp.bfloat16)
    source = lax.broadcasted_iota(jnp.int32, (DISC, LANES), 0)
    target = lax.broadcasted_iota(jnp.int32, (DISC, LANES), 1)
    mirror = jnp.where((source + target) % LANES == 0, 1.0, 0.0).astype(jnp.bfloat16)
    mirrored = jnp.dot(kernel, mirror, preferred_element_type=jnp.float32)
    left = lax.broadcasted_iota(jnp.int32, (LANES, LANES), 1) < SPAN

    def band(row, start):
        wide = jnp.broadcast_to(mirrored[row : row + 1, :], (LANES, LANES))
        return pltpu.roll(wide, start, 1, stride=1, stride_axis=0)

    for u in range(TURNS):
        for s in range(0, STEP, 2):
            row = u * STEP + s
            both = jnp.where(left, band(row, 0), band(row + 1, SPAN))
            pairs_ref[u * LANES : (u + 1) * LANES, s * SPAN : (s + 2) * SPAN] = both.astype(jnp.bfloat16)
    last_ref[...] = jnp.where(left, band(2 * HALO, 0), 0.0).astype(jnp.bfloat16)


def hats(row, cell):
    near, far, here, there = (value.astype(jnp.bfloat16) for value in row)
    zero = jnp.zeros((), jnp.bfloat16)
    return jnp.where(cell == here, near, jnp.where(cell == there, far, zero))


def deposited(both, lists, stage, shifts, facts):
    sources = both.shape[0]
    rays = 3 * LANES
    first_lane = lax.axis_index("row") % 2 * 8
    room = sources * ROOM + 1
    lane = lax.broadcasted_iota(jnp.int32, (sources, LANES), 1)
    parity = lax.axis_index("row") % 2
    words = jnp.where(lane == KINDS + parity, both[:, 7, 2 * LANES :][:, :LANES], 0.0)
    words = jnp.sum(words, axis=1, keepdims=True).astype(jnp.int32)
    words = [words[at, 0] for at in range(sources)]

    def listed(counts, kinds, slots):
        counts = list(counts)
        for kind in kinds:
            for at in range(sources):
                for k in slots:
                    lists[kind * room + counts[kind]] = at * 8 + k
                    bit = (words[at] >> (ROOM * kind + k)) & 1
                    counts[kind] = counts[kind] + bit
        return tuple(counts)

    counts = (jnp.int32(0),) * 4
    used = functools.reduce(jnp.bitwise_or, words)
    for slot in range(COMMON, ROOM):
        counts = lax.cond(
            used & sum(1 << (ROOM * kind + slot) for kind in range(4)) != 0,
            lambda held, slot=slot: listed(held, range(4), (slot,)),
            lambda held: held,
            counts,
        )

    def doubled(cell):
        return (2 * cell).astype(jnp.float32).astype(jnp.bfloat16)

    own = doubled(lax.broadcasted_iota(jnp.int32, (TILE, rays), 0))
    edge = lax.broadcasted_iota(jnp.int32, (2 * HALO, rays), 0)
    edge = doubled(jnp.where(edge < HALO, edge - HALO, edge + (TILE - HALO)))
    lane = lax.broadcasted_iota(jnp.int32, (1, LANES), 1) - first_lane

    def load(kind, step, batch, start):
        for k in range(batch):
            at = start + k
            entry = lists[kind * room + jnp.minimum(step * batch + k, counts[kind])]
            source, slot = entry >> 3, entry & 7
            head = both[source, pl.ds(slot, 1), :]
            tail = both[source, pl.ds(ROOM + (slot >> 1), 1), :]
            meta = both[source, 7:8, :][:, 2 * LANES : 3 * LANES]
            stage[0, at : at + 1, :] = head[:, :rays]
            stage[1, at : at + 1, :LANES] = head[:, rays:]
            stage[1, at : at + 1, LANES:] = jnp.where(
                (slot & 1) == 1, tail[:, 2 * LANES :], tail[:, : 2 * LANES]
            )
            shifts[at : at + 1, :] = jnp.where(lane == slot, meta, 0.0)

    def prepare(begin, end):
        code = jnp.sum(shifts[begin:end, :], axis=1, keepdims=True)
        rowwise = jnp.floor((code + 0.5) / 3.0)
        offsets = (rowwise - 1.0) * (2.0 * TILE), (code - 3.0 * rowwise - 1.0) * (2.0 * TILE)
        for axis in range(2):
            coords = stage[axis, begin:end, :]
            low = jnp.floor(coords)
            facts[4 * axis, begin:end, :] = 1.0 - (coords - low)
            facts[4 * axis + 1, begin:end, :] = 1.0 - ((low + 1.0) - coords)
            here = 2.0 * low + offsets[axis]
            facts[4 * axis + 2, begin:end, :] = here
            facts[4 * axis + 3, begin:end, :] = here + 2.0

    def product(kind, batch, start):
        down, across = (own, edge)[kind // 2], (own, edge)[kind % 2]
        firsts, seconds = [], []
        for at in range(start, start + batch):
            row = [facts[j, at : at + 1, :] for j in range(8)]
            firsts.append(hats(row[:4], down))
            seconds.append(hats(row[4:], across))
        return lax.dot_general(
            jnp.concatenate(firsts, axis=1),
            jnp.concatenate(seconds, axis=1),
            (((1,), (1,)), ((), ())),
            preferred_element_type=jnp.float32,
        )

    def ready(step, *given):
        for kind, batch, start in given:
            load(kind, step, batch, start)
        prepare(given[0][2], given[-1][2] + BATCH)

    def together(one, two):
        def step_one(step, sums, given=one):
            sums = sums + product(*given)
            ready(step + 1, given)
            return sums

        def step_both(step, sums):
            sums = sums[0] + product(*one), sums[1] + product(*two)
            ready(step + 1, one, two)
            return sums

        zeros = [
            jnp.zeros(((TILE, 2 * HALO)[kind // 2], (TILE, 2 * HALO)[kind % 2]), jnp.float32)
            for kind in (one[0], two[0])
        ]
        steps = [(counts[kind] + batch - 1) // batch for kind, batch, _ in (one, two)]
        shared = jnp.minimum(steps[0], steps[1])
        sums = lax.fori_loop(0, shared, step_both, tuple(zeros))
        return [
            lax.fori_loop(shared, steps[j], functools.partial(step_one, given=(one, two)[j]), sums[j])
            for j in range(2)
        ]

    pairs = (
        ((0, 6, 0), (3, 3, BATCH)),
        ((1, BATCH // 2, 2 * BATCH), (2, BATCH // 2, 3 * BATCH)),
    )
    for pair in pairs:
        kinds = [kind for kind, _, _ in pair]
        counts = listed(counts, kinds, range(COMMON))
        for kind in kinds:
            lists[kind * room + counts[kind]] = ROOM
        ready(0, *pair)
    inside, corners = together(*pairs[0])
    beside, above = together(*pairs[1])

    def wide(middle, ends):
        return jnp.concatenate([ends[:, :HALO], middle, ends[:, HALO:]], axis=1)

    middle, ends = wide(inside, beside), wide(above, corners)
    return jnp.concatenate([ends[:HALO], middle, ends[HALO:]], axis=0)


def spread_kernel(scale, mine_ref, other_ref, before_ref, pairs_ref, last_ref, out_ref, total_ref,
                  left, both, *scratch):
    sources = mine_ref.shape[0]
    both[:sources] = mine_ref[...]
    both[sources:] = other_ref[...]
    cells = deposited(both, *scratch)
    if before_ref is not None:
        cells = cells + before_ref[...]
    total_ref[...] = cells
    blocks = [cells[:, at : at + LANES].astype(jnp.bfloat16) for at in (0, SPAN)]
    for h in range(2):
        for u in range(TURNS):
            left[h * LONG : (h + 1) * LONG, u * LANES : (u + 1) * LANES] = blocks[h][
                u * STEP : u * STEP + LONG, :
            ]
    lowest = jnp.concatenate([block[2 * HALO :, :] for block in blocks], axis=0)
    ends = jnp.dot(lowest, last_ref[...], preferred_element_type=jnp.float32)
    evens = [ends[:TILE], ends[TILE:]]
    odds = [jnp.zeros((TILE, LANES), jnp.float32)] * 2
    for p in range(0, STEP * SPAN, 2 * LANES):
        both = jnp.dot(left[...], pairs_ref[:, p : p + 2 * LANES], preferred_element_type=jnp.float32)
        for h in range(2):
            for lanes in (0, LANES):
                s = (p + lanes) // SPAN
                part = both[h * LONG : (h + 1) * LONG, lanes : lanes + LANES]
                evens[h] = evens[h] + part[s : s + TILE]
                odds[h] = odds[h] + part[s + 1 : s + 1 + TILE]
    low = evens[0] + pltpu.roll(odds[0], SPAN, 1)
    high = pltpu.roll(evens[1], SPAN, 1) + odds[1]
    lane = lax.broadcasted_iota(jnp.int32, (TILE, LANES), 1)
    out_ref[...] = jnp.where(lane < SPAN, low, high) / scale


def shards(positions, destination, profile):
    blocks, _, rays = positions.shape
    row_count, col_count = lax.axis_size("row"), lax.axis_size("col")
    tiles = row_count * col_count
    width = -(-(3 * blocks + tiles) // LANES) * LANES

    def exchange(turn, labels, coords):
        kernel, given = pack_kernel, (turn, labels, coords)
        if turn is None:
            kernel, given = functools.partial(pack_kernel, None), (labels, coords)
        outgoing = pl.pallas_call(
            kernel,
            out_shape=jax.ShapeDtypeStruct((8 * tiles, rays + LANES), jnp.float32),
            in_specs=[SMEM, VMEM, VMEM][-len(given) :],
            out_specs=VMEM,
            scratch_shapes=[
                pltpu.VMEM((1, width), jnp.float32),
                pltpu.VMEM((width, rays + LANES), jnp.float32),
            ],
            compiler_params=ALONE if turn is None else LIMIT,
            name="pack",
        )(*given)
        return lax.all_to_all(
            outgoing.reshape(tiles, 8, rays + LANES), ("row", "col"), split_axis=0, concat_axis=0, tiled=True
        )

    def deposit(mine, before, pairs, last):
        other = lax.ppermute(mine, "row", [(i, i ^ 1) for i in range(row_count)])
        scale = blocks * rays / (TILE * TILE)
        kernel, given = functools.partial(spread_kernel, scale), (mine, other, before, pairs, last)
        if before is None:
            kernel = lambda mine, other, *refs: spread_kernel(scale, mine, other, None, *refs)
            given = (mine, other, pairs, last)
        return pl.pallas_call(
            kernel,
            out_shape=(
                jax.ShapeDtypeStruct((TILE, TILE), jnp.float32),
                jax.ShapeDtypeStruct((WIDE, WIDE), jnp.float32),
            ),
            in_specs=[VMEM] * len(given),
            out_specs=(VMEM, VMEM),
            scratch_shapes=[
                pltpu.VMEM((2 * LONG, TURNS * LANES), jnp.bfloat16),
                pltpu.VMEM((2 * tiles, 8, rays + LANES), jnp.float32),
                pltpu.SMEM((4 * (2 * tiles * ROOM + 1),), jnp.int32),
                pltpu.VMEM((2, 4 * BATCH, rays), jnp.float32),
                pltpu.VMEM((4 * BATCH, LANES), jnp.float32),
                pltpu.VMEM((8, 4 * BATCH, rays), jnp.float32),
            ],
            compiler_params=LIMIT,
            name="spread",
        )(*given)

    mine = exchange(None, destination.T, positions)
    pairs, last, labels, coords = pl.pallas_call(
        table_kernel,
        out_shape=(
            jax.ShapeDtypeStruct((TURNS * LANES, STEP * SPAN), jnp.bfloat16),
            jax.ShapeDtypeStruct((LANES, LANES), jnp.bfloat16),
            jax.ShapeDtypeStruct((1, blocks), jnp.int32),
            jax.ShapeDtypeStruct(positions.shape, jnp.float32),
        ),
        in_specs=[VMEM] * 3,
        out_specs=(VMEM,) * 4,
        compiler_params=LIMIT,
        cost_estimate=pl.CostEstimate(flops=10_000_000, bytes_accessed=6_000_000, transcendentals=0),
        name="table",
    )(profile, destination.T, positions)
    mine, pairs, last, labels, coords = lax.optimization_barrier((mine, pairs, last, labels, coords))
    turns = jnp.max(mine[:, 7, 2 * LANES + COUNT]).astype(jnp.int32)
    out, total = deposit(mine, None, pairs, last)

    def more(state):
        turn, _, total = state
        out, total = deposit(
            exchange(jnp.full((1,), turn, jnp.int32), labels, coords), total, pairs, last
        )
        return turn + 1, out, total

    return lax.while_loop(lambda state: state[0] < turns, more, (jnp.int32(1), out, total))[1]


def solution(mesh):
    placed = (P(("maps", "row", "col"), None, None), P(("maps", "row", "col"), None), P())
    return jax.shard_map(
        shards, mesh=mesh, in_specs=placed, out_specs=P(("maps", "row"), "col"), check_vma=False
    )
```

profile of v0, /device:TPU:1, one launch (start us, length us, event | category | flops | bytes accessed | tf_op | source)
XLA Modules:
  0.0 26.4 jit_solution(5524404135169524849)
XLA Ops:
  0.0 2.2 %pack.2 = f32[128,512]{1,0:T(8,128)} custom-call(s32[1,16]{1,0:T(1,128)} %bitcast.9, f32[16,2,384]{2,1,0:T(2,128)} %rays_ref.3), custom_call_target="tpu_custom_call" | custom-call | tf_op jit(solution)/shard_map/pack/pallas_call | solution.py:336
  2.2 0.0 copy-start
  2.2 0.0 copy-start.1
  2.2 0.0 copy-start.2
  2.2 7.5 %all-to-all-start.1 = ((f32[16,8,512]{2,1,0:T(8,128)}), f32[16,8,512]{2,1,0:T(8,128)S(1)}, u32[]{:S(2)}, u32[]{:S(2)}) async-start(f32[16,8,512]{2,1,0:T(8,128)} %bitcast.11), calls=%async_computation.1 | async-start | bytes 524288 | tf_op jit(solution)/shard_map/all_to_all | solution.py:348
  9.6 0.0 copy-done
  9.6 0.0 copy-done.1
  9.7 0.0 copy-done.2
  9.7 0.9 %table.1 = (bf16[512,1024]{1,0:T(8,128)(2,1)S(1)}, bf16[128,128]{1,0:T(8,128)(2,1)S(1)}, s32[1,16]{1,0:T(1,128)S(1)}, f32[16,2,384]{2,1,0:T(2,128)S(1)}) custom-call(f32[65,65]{1,0:T(8,128)S(1)} %copy-done.1, s32[1,16]{1,0:T(1,128)S(1)} %bitcast.10, f32[16,2,384]{2,1,0:T(2,128)S(1)} %copy-done), custom_call_target="tpu_custom_call" | custom-call | flops 10000000 | bytes 6000000 | tf_op jit(solution)/shard_map/table/pallas_call | solution.py:380
  10.6 8.4 %all-to-all-done.1.mine = f32[16,8,512]{2,1,0:T(8,128)S(1)} async-done(((f32[16,8,512]{2,1,0:T(8,128)}), f32[16,8,512]{2,1,0:T(8,128)S(1)}, u32[]{:S(2)}, u32[]{:S(2)}) %all-to-all-start.1) | async-done | bytes 262176 | tf_op jit(solution)/shard_map/all_to_all | solution.py:348
  19.0 0.8 %collective-permute-start.1 = (f32[16,8,512]{2,1,0:T(8,128)S(1)}, f32[16,8,512]{2,1,0:T(8,128)S(1)}, u32[]{:S(2)}, u32[]{:S(2)}) collective-permute-start(f32[16,8,512]{2,1,0:T(8,128)S(1)} %all-to-all-done.1.mine), channel_id=1, source_target_pairs={{0,4},{4,0},{8,12},{12,8},{1,5},{5,1},{9,13},{13,9},{2,6},{6,2},{1... | collective-permute-start | bytes 786440 | tf_op jit(solution)/shard_map/ppermute | solution.py:353
  19.8 0.7 %slice_reduce_fusion = f32[]{:T(128)} fusion(f32[16,8,512]{2,1,0:T(8,128)S(1)} %all-to-all-done.1.mine), kind=kLoop, calls=%fused_computation | loop fusion | flops 15 | bytes 68 | tf_op jit(solution)/shard_map/reduce_max | solution.py:395
  21.1 0.0 collective-permute-done.1.other
  21.2 5.2 %spread.2 = (f32[128,128]{1,0:T(8,128)}, f32[192,192]{1,0:T(8,128)S(1)}) custom-call(f32[16,8,512]{2,1,0:T(8,128)S(1)} %all-to-all-done.1.mine, f32[16,8,512]{2,1,0:T(8,128)S(1)} %collective-permute-done.1.other, bf16[512,1024]{1,0:T(8,128)(2,1)S(1)} %get-tuple-element.146.refs_0_, bf16[128,128]{1,0:T(8,128)(2,1)S(1)} %get-tuple-element.147.refs_1_), custom_call_target="tpu_custom_call" | custom-call | tf_op jit(solution)/shard_map/spread/pallas_call | solution.py:359
  (1 shorter events, 0.0 us)
Async XLA Ops:
  2.2 7.5 %copy-start = (f32[16,2,384]{2,1,0:T(2,128)S(1)}, f32[16,2,384]{2,1,0:T(2,128)}, u32[]{:S(2)}) copy-start(f32[16,2,384]{2,1,0:T(2,128)} %rays_ref.3) | copy-start | bytes 147460
  2.2 7.5 %copy-start.1 = (f32[65,65]{1,0:T(8,128)S(1)}, f32[65,65]{1,0:T(8,128)}, u32[]{:S(2)}) copy-start(f32[65,65]{1,0:T(8,128)} %profile_ref.1) | copy-start | bytes 50704
  2.2 7.5 %copy-start.2 = (s32[16,1]{0,1:T(1,128)S(1)}, s32[16,1]{0,1:T(1,128)}, u32[]{:S(2)}) copy-start(s32[16,1]{0,1:T(1,128)} %param.6) | copy-start | bytes 196
  2.2 16.8 %all-to-all-start.1 = ((f32[16,8,512]{2,1,0:T(8,128)}), f32[16,8,512]{2,1,0:T(8,128)S(1)}, u32[]{:S(2)}, u32[]{:S(2)}) async-start(f32[16,8,512]{2,1,0:T(8,128)} %bitcast.11), calls=%async_computation.1 | async-start | bytes 524288 | tf_op jit(solution)/shard_map/all_to_all | solution.py:348
  19.0 2.2 %collective-permute-start.1 = (f32[16,8,512]{2,1,0:T(8,128)S(1)}, f32[16,8,512]{2,1,0:T(8,128)S(1)}, u32[]{:S(2)}, u32[]{:S(2)}) collective-permute-start(f32[16,8,512]{2,1,0:T(8,128)S(1)} %all-to-all-done.1.mine), channel_id=1, source_target_pairs={{0,4},{4,0},{8,12},{12,8},{1,5},{5,1},{9,13},{13,9},{2,6},{6,2},{1... | collective-permute-start | bytes 786440 | tf_op jit(solution)/shard_map/ppermute | solution.py:353
where the time goes:
time: 26.6 us; the launch traced here: 26.4 us
  waiting for transfers between devices  8.44 us (32%)
  Pallas kernels  8.27 us (31%)
  starting transfers between devices  8.27 us (31%)
  other arithmetic  0.69 us (3%)
  between operations  0.69 us (3%)
    all_to_all x1, waiting for transfers between devices, exchange(): lax.all_to_all(outgoing.reshape(tiles, 8, rays + LANES), ('row', 'col'),...  8.43 us
    all_to_all x1, starting transfers between devices, exchange(): lax.all_to_all(outgoing.reshape(tiles, 8, rays + LANES), ('row', 'col'),...  7.45 us
    pallas_call x1, Pallas kernels, deposit(): pl.pallas_call(kernel, out_shape=(jax.ShapeDtypeStruct((TILE, TILE), jnp....  5.21 us
    pallas_call x1, Pallas kernels, exchange(): pl.pallas_call(kernel, out_shape=jax.ShapeDtypeStruct((8 * tiles, rays +...  2.18 us
    pallas_call x1, Pallas kernels, shards(): pl.pallas_call(table_kernel, out_shape=(jax.ShapeDtypeStruct((TURNS * LAN...  0.88 us
    ppermute x1, starting transfers between devices, deposit(): other = lax.ppermute(mine, 'row', [(i, i ^ 1) for i in range(row_count)])  0.82 us
    reduce_max x1, other arithmetic, shards(): turns = jnp.max(mine[:, 7, 2 * LANES + COUNT]).astype(jnp.int32)  0.69 us
  transfers between devices with their start and end apart: 2, of which 1 were waited for; matrix products, arithmetic and copies ran while one was open for 3% of the time, Pallas kernels for 3%

commit v1 on v0

--- a/solution.py
+++ b/solution.py
@@ -177,12 +177,12 @@
         for kind in kinds:
             for at in range(sources):
                 for k in slots:
-                    lists[kind * room + counts[kind]] = at * 8 + k
+                    lists[counts[kind]] = at * 8 + k
                     bit = (words[at] >> (ROOM * kind + k)) & 1
                     counts[kind] = counts[kind] + bit
         return tuple(counts)
 
-    counts = (jnp.int32(0),) * 4
+    counts = tuple(jnp.int32(kind * room) for kind in range(4))
     used = functools.reduce(jnp.bitwise_or, words)
     for slot in range(COMMON, ROOM):
         counts = lax.cond(
@@ -203,7 +203,7 @@
     def load(kind, step, batch, start):
         for k in range(batch):
             at = start + k
-            entry = lists[kind * room + jnp.minimum(step * batch + k, counts[kind])]
+            entry = lists[jnp.minimum(kind * room + k + step * batch, counts[kind])]
             source, slot = entry >> 3, entry & 7
             head = both[source, pl.ds(slot, 1), :]
             tail = both[source, pl.ds(ROOM + (slot >> 1), 1), :]
@@ -262,7 +262,7 @@
             jnp.zeros(((TILE, 2 * HALO)[kind // 2], (TILE, 2 * HALO)[kind % 2]), jnp.float32)
             for kind in (one[0], two[0])
         ]
-        steps = [(counts[kind] + batch - 1) // batch for kind, batch, _ in (one, two)]
+        steps = [(counts[kind] - kind * room + batch - 1) // batch for kind, batch, _ in (one, two)]
         shared = jnp.minimum(steps[0], steps[1])
         sums = lax.fori_loop(0, shared, step_both, tuple(zeros))
         return [
@@ -271,14 +271,14 @@
         ]
 
     pairs = (
-        ((0, 6, 0), (3, 3, BATCH)),
+        ((0, BATCH, 0), (3, BATCH // 2, BATCH)),
         ((1, BATCH // 2, 2 * BATCH), (2, BATCH // 2, 3 * BATCH)),
     )
     for pair in pairs:
         kinds = [kind for kind, _, _ in pair]
         counts = listed(counts, kinds, range(COMMON))
         for kind in kinds:
-            lists[kind * room + counts[kind]] = ROOM
+            lists[counts[kind]] = ROOM
         ready(0, *pair)
     inside, corners = together(*pairs[0])
     beside, above = together(*pairs[1])

time: 26.6 us -> 27.4 us (1.030)
  Pallas kernels: 8.27 us -> 9 us
    pallas_call x1, Pallas kernels: 5.21 us -> 5.94 us  [deposit(): pl.pallas_call(kernel, out_shape=(jax.ShapeDtypeStruct((TILE, TILE), jnp....]
where the time goes in v1:
time: 27.4 us; the launch traced here: 27.1 us
  Pallas kernels  9 us (33%)
  waiting for transfers between devices  8.44 us (31%)
  starting transfers between devices  8.27 us (30%)
  other arithmetic  0.69 us (3%)
  between operations  0.69 us (3%)
    all_to_all x1, waiting for transfers between devices, exchange(): lax.all_to_all(outgoing.reshape(tiles, 8, rays + LANES), ('row', 'col'),...  8.43 us
    all_to_all x1, starting transfers between devices, exchange(): lax.all_to_all(outgoing.reshape(tiles, 8, rays + LANES), ('row', 'col'),...  7.45 us
    pallas_call x1, Pallas kernels, deposit(): pl.pallas_call(kernel, out_shape=(jax.ShapeDtypeStruct((TILE, TILE), jnp....  5.94 us
    pallas_call x1, Pallas kernels, exchange(): pl.pallas_call(kernel, out_shape=jax.ShapeDtypeStruct((8 * tiles, rays +...  2.18 us
    pallas_call x1, Pallas kernels, shards(): pl.pallas_call(table_kernel, out_shape=(jax.ShapeDtypeStruct((TURNS * LAN...  0.88 us
    ppermute x1, starting transfers between devices, deposit(): other = lax.ppermute(mine, 'row', [(i, i ^ 1) for i in range(row_count)])  0.82 us
    reduce_max x1, other arithmetic, shards(): turns = jnp.max(mine[:, 7, 2 * LANES + COUNT]).astype(jnp.int32)  0.69 us
  transfers between devices with their start and end apart: 2, of which 1 were waited for; matrix products, arithmetic and copies ran while one was open for 3% of the time, Pallas kernels for 3%

profile of v1, /device:TPU:1, one launch (start us, length us, event | category | flops | bytes accessed | tf_op | source)
XLA Modules:
  0.0 27.1 jit_solution(8946360660156643125)
XLA Ops:
  0.0 2.2 %pack.2 = f32[128,512]{1,0:T(8,128)} custom-call(s32[1,16]{1,0:T(1,128)} %bitcast.9, f32[16,2,384]{2,1,0:T(2,128)} %rays_ref.3), custom_call_target="tpu_custom_call" | custom-call | tf_op jit(solution)/shard_map/pack/pallas_call | solution.py:336
  2.2 0.0 copy-start
  2.2 0.0 copy-start.1
  2.2 0.0 copy-start.2
  2.2 7.5 %all-to-all-start.1 = ((f32[16,8,512]{2,1,0:T(8,128)}), f32[16,8,512]{2,1,0:T(8,128)S(1)}, u32[]{:S(2)}, u32[]{:S(2)}) async-start(f32[16,8,512]{2,1,0:T(8,128)} %bitcast.11), calls=%async_computation.1 | async-start | bytes 524288 | tf_op jit(solution)/shard_map/all_to_all | solution.py:348
  9.6 0.0 copy-done
  9.6 0.0 copy-done.1
  9.7 0.0 copy-done.2
  9.7 0.9 %table.1 = (bf16[512,1024]{1,0:T(8,128)(2,1)S(1)}, bf16[128,128]{1,0:T(8,128)(2,1)S(1)}, s32[1,16]{1,0:T(1,128)S(1)}, f32[16,2,384]{2,1,0:T(2,128)S(1)}) custom-call(f32[65,65]{1,0:T(8,128)S(1)} %copy-done.1, s32[1,16]{1,0:T(1,128)S(1)} %bitcast.10, f32[16,2,384]{2,1,0:T(2,128)S(1)} %copy-done), custom_call_target="tpu_custom_call" | custom-call | flops 10000000 | bytes 6000000 | tf_op jit(solution)/shard_map/table/pallas_call | solution.py:380
  10.6 8.4 %all-to-all-done.1.mine = f32[16,8,512]{2,1,0:T(8,128)S(1)} async-done(((f32[16,8,512]{2,1,0:T(8,128)}), f32[16,8,512]{2,1,0:T(8,128)S(1)}, u32[]{:S(2)}, u32[]{:S(2)}) %all-to-all-start.1) | async-done | bytes 262176 | tf_op jit(solution)/shard_map/all_to_all | solution.py:348
  19.0 0.8 %collective-permute-start.1 = (f32[16,8,512]{2,1,0:T(8,128)S(1)}, f32[16,8,512]{2,1,0:T(8,128)S(1)}, u32[]{:S(2)}, u32[]{:S(2)}) collective-permute-start(f32[16,8,512]{2,1,0:T(8,128)S(1)} %all-to-all-done.1.mine), channel_id=1, source_target_pairs={{0,4},{4,0},{8,12},{12,8},{1,5},{5,1},{9,13},{13,9},{2,6},{6,2},{1... | collective-permute-start | bytes 786440 | tf_op jit(solution)/shard_map/ppermute | solution.py:353
  19.8 0.7 %slice_reduce_fusion = f32[]{:T(128)} fusion(f32[16,8,512]{2,1,0:T(8,128)S(1)} %all-to-all-done.1.mine), kind=kLoop, calls=%fused_computation | loop fusion | flops 15 | bytes 68 | tf_op jit(solution)/shard_map/reduce_max | solution.py:395
  21.1 0.0 collective-permute-done.1.other
  21.2 5.9 %spread.2 = (f32[128,128]{1,0:T(8,128)}, f32[192,192]{1,0:T(8,128)S(1)}) custom-call(f32[16,8,512]{2,1,0:T(8,128)S(1)} %all-to-all-done.1.mine, f32[16,8,512]{2,1,0:T(8,128)S(1)} %collective-permute-done.1.other, bf16[512,1024]{1,0:T(8,128)(2,1)S(1)} %get-tuple-element.146.refs_0_, bf16[128,128]{1,0:T(8,128)(2,1)S(1)} %get-tuple-element.147.refs_1_), custom_call_target="tpu_custom_call" | custom-call | tf_op jit(solution)/shard_map/spread/pallas_call | solution.py:359
  (1 shorter events, 0.0 us)
Async XLA Ops:
  2.2 7.5 %copy-start = (f32[16,2,384]{2,1,0:T(2,128)S(1)}, f32[16,2,384]{2,1,0:T(2,128)}, u32[]{:S(2)}) copy-start(f32[16,2,384]{2,1,0:T(2,128)} %rays_ref.3) | copy-start | bytes 147460
  2.2 7.5 %copy-start.1 = (f32[65,65]{1,0:T(8,128)S(1)}, f32[65,65]{1,0:T(8,128)}, u32[]{:S(2)}) copy-start(f32[65,65]{1,0:T(8,128)} %profile_ref.1) | copy-start | bytes 50704
  2.2 7.5 %copy-start.2 = (s32[16,1]{0,1:T(1,128)S(1)}, s32[16,1]{0,1:T(1,128)}, u32[]{:S(2)}) copy-start(s32[16,1]{0,1:T(1,128)} %param.6) | copy-start | bytes 196
  2.2 16.8 %all-to-all-start.1 = ((f32[16,8,512]{2,1,0:T(8,128)}), f32[16,8,512]{2,1,0:T(8,128)S(1)}, u32[]{:S(2)}, u32[]{:S(2)}) async-start(f32[16,8,512]{2,1,0:T(8,128)} %bitcast.11), calls=%async_computation.1 | async-start | bytes 524288 | tf_op jit(solution)/shard_map/all_to_all | solution.py:348
  19.0 2.2 %collective-permute-start.1 = (f32[16,8,512]{2,1,0:T(8,128)S(1)}, f32[16,8,512]{2,1,0:T(8,128)S(1)}, u32[]{:S(2)}, u32[]{:S(2)}) collective-permute-start(f32[16,8,512]{2,1,0:T(8,128)S(1)} %all-to-all-done.1.mine), channel_id=1, source_target_pairs={{0,4},{4,0},{8,12},{12,8},{1,5},{5,1},{9,13},{13,9},{2,6},{6,2},{1... | collective-permute-start | bytes 786440 | tf_op jit(solution)/shard_map/ppermute | solution.py:353

commit v2 on v1

--- a/solution.py
+++ b/solution.py
@@ -272,7 +272,7 @@
 
     pairs = (
         ((0, BATCH, 0), (3, BATCH // 2, BATCH)),
-        ((1, BATCH // 2, 2 * BATCH), (2, BATCH // 2, 3 * BATCH)),
+        ((1, 6, 2 * BATCH), (2, 6, 3 * BATCH)),
     )
     for pair in pairs:
         kinds = [kind for kind, _, _ in pair]

time: 27.4 us -> 26.4 us (0.964); the launches traced: 27.1 us -> 26.4 us
  Pallas kernels: 9 us -> 8.29 us
    pallas_call x1, Pallas kernels: 5.94 us -> 5.23 us  [deposit(): pl.pallas_call(kernel, out_shape=(jax.ShapeDtypeStruct((TILE, TILE), jnp....]
where the time goes in v2:
time: 26.4 us
  waiting for transfers between devices  8.44 us (32%)
  Pallas kernels  8.29 us (31%)
  starting transfers between devices  8.27 us (31%)
  other arithmetic  0.69 us (3%)
  between operations  0.69 us (3%)
    all_to_all x1, waiting for transfers between devices, exchange(): lax.all_to_all(outgoing.reshape(tiles, 8, rays + LANES), ('row', 'col'),...  8.43 us
    all_to_all x1, starting transfers between devices, exchange(): lax.all_to_all(outgoing.reshape(tiles, 8, rays + LANES), ('row', 'col'),...  7.45 us
    pallas_call x1, Pallas kernels, deposit(): pl.pallas_call(kernel, out_shape=(jax.ShapeDtypeStruct((TILE, TILE), jnp....  5.23 us
    pallas_call x1, Pallas kernels, exchange(): pl.pallas_call(kernel, out_shape=jax.ShapeDtypeStruct((8 * tiles, rays +...  2.18 us
    pallas_call x1, Pallas kernels, shards(): pl.pallas_call(table_kernel, out_shape=(jax.ShapeDtypeStruct((TURNS * LAN...  0.88 us
    ppermute x1, starting transfers between devices, deposit(): other = lax.ppermute(mine, 'row', [(i, i ^ 1) for i in range(row_count)])  0.82 us
    reduce_max x1, other arithmetic, shards(): turns = jnp.max(mine[:, 7, 2 * LANES + COUNT]).astype(jnp.int32)  0.69 us
  transfers between devices with their start and end apart: 2, of which 1 were waited for; matrix products, arithmetic and copies ran while one was open for 3% of the time, Pallas kernels for 3%

profile of v2, /device:TPU:1, one launch (start us, length us, event | category | flops | bytes accessed | tf_op | source)
XLA Modules:
  0.0 26.4 jit_solution(7761732109562620095)
XLA Ops:
  0.0 2.2 %pack.2 = f32[128,512]{1,0:T(8,128)} custom-call(s32[1,16]{1,0:T(1,128)} %bitcast.9, f32[16,2,384]{2,1,0:T(2,128)} %rays_ref.3), custom_call_target="tpu_custom_call" | custom-call | tf_op jit(solution)/shard_map/pack/pallas_call | solution.py:336
  2.2 0.0 copy-start
  2.2 0.0 copy-start.1
  2.2 0.0 copy-start.2
  2.2 7.5 %all-to-all-start.1 = ((f32[16,8,512]{2,1,0:T(8,128)}), f32[16,8,512]{2,1,0:T(8,128)S(1)}, u32[]{:S(2)}, u32[]{:S(2)}) async-start(f32[16,8,512]{2,1,0:T(8,128)} %bitcast.11), calls=%async_computation.1 | async-start | bytes 524288 | tf_op jit(solution)/shard_map/all_to_all | solution.py:348
  9.6 0.0 copy-done
  9.6 0.0 copy-done.1
  9.7 0.0 copy-done.2
  9.7 0.9 %table.1 = (bf16[512,1024]{1,0:T(8,128)(2,1)S(1)}, bf16[128,128]{1,0:T(8,128)(2,1)S(1)}, s32[1,16]{1,0:T(1,128)S(1)}, f32[16,2,384]{2,1,0:T(2,128)S(1)}) custom-call(f32[65,65]{1,0:T(8,128)S(1)} %copy-done.1, s32[1,16]{1,0:T(1,128)S(1)} %bitcast.10, f32[16,2,384]{2,1,0:T(2,128)S(1)} %copy-done), custom_call_target="tpu_custom_call" | custom-call | flops 10000000 | bytes 6000000 | tf_op jit(solution)/shard_map/table/pallas_call | solution.py:380
  10.6 8.4 %all-to-all-done.1.mine = f32[16,8,512]{2,1,0:T(8,128)S(1)} async-done(((f32[16,8,512]{2,1,0:T(8,128)}), f32[16,8,512]{2,1,0:T(8,128)S(1)}, u32[]{:S(2)}, u32[]{:S(2)}) %all-to-all-start.1) | async-done | bytes 262176 | tf_op jit(solution)/shard_map/all_to_all | solution.py:348
  19.0 0.8 %collective-permute-start.1 = (f32[16,8,512]{2,1,0:T(8,128)S(1)}, f32[16,8,512]{2,1,0:T(8,128)S(1)}, u32[]{:S(2)}, u32[]{:S(2)}) collective-permute-start(f32[16,8,512]{2,1,0:T(8,128)S(1)} %all-to-all-done.1.mine), channel_id=1, source_target_pairs={{0,4},{4,0},{8,12},{12,8},{1,5},{5,1},{9,13},{13,9},{2,6},{6,2},{1... | collective-permute-start | bytes 786440 | tf_op jit(solution)/shard_map/ppermute | solution.py:353
  19.8 0.7 %slice_reduce_fusion = f32[]{:T(128)} fusion(f32[16,8,512]{2,1,0:T(8,128)S(1)} %all-to-all-done.1.mine), kind=kLoop, calls=%fused_computation | loop fusion | flops 15 | bytes 68 | tf_op jit(solution)/shard_map/reduce_max | solution.py:395
  21.1 0.0 collective-permute-done.1.other
  21.2 5.2 %spread.2 = (f32[128,128]{1,0:T(8,128)}, f32[192,192]{1,0:T(8,128)S(1)}) custom-call(f32[16,8,512]{2,1,0:T(8,128)S(1)} %all-to-all-done.1.mine, f32[16,8,512]{2,1,0:T(8,128)S(1)} %collective-permute-done.1.other, bf16[512,1024]{1,0:T(8,128)(2,1)S(1)} %get-tuple-element.146.refs_0_, bf16[128,128]{1,0:T(8,128)(2,1)S(1)} %get-tuple-element.147.refs_1_), custom_call_target="tpu_custom_call" | custom-call | tf_op jit(solution)/shard_map/spread/pallas_call | solution.py:359
  (1 shorter events, 0.0 us)
Async XLA Ops:
  2.2 7.5 %copy-start = (f32[16,2,384]{2,1,0:T(2,128)S(1)}, f32[16,2,384]{2,1,0:T(2,128)}, u32[]{:S(2)}) copy-start(f32[16,2,384]{2,1,0:T(2,128)} %rays_ref.3) | copy-start | bytes 147460
  2.2 7.5 %copy-start.1 = (f32[65,65]{1,0:T(8,128)S(1)}, f32[65,65]{1,0:T(8,128)}, u32[]{:S(2)}) copy-start(f32[65,65]{1,0:T(8,128)} %profile_ref.1) | copy-start | bytes 50704
  2.2 7.5 %copy-start.2 = (s32[16,1]{0,1:T(1,128)S(1)}, s32[16,1]{0,1:T(1,128)}, u32[]{:S(2)}) copy-start(s32[16,1]{0,1:T(1,128)} %param.6) | copy-start | bytes 196
  2.2 16.8 %all-to-all-start.1 = ((f32[16,8,512]{2,1,0:T(8,128)}), f32[16,8,512]{2,1,0:T(8,128)S(1)}, u32[]{:S(2)}, u32[]{:S(2)}) async-start(f32[16,8,512]{2,1,0:T(8,128)} %bitcast.11), calls=%async_computation.1 | async-start | bytes 524288 | tf_op jit(solution)/shard_map/all_to_all | solution.py:348
  19.0 2.2 %collective-permute-start.1 = (f32[16,8,512]{2,1,0:T(8,128)S(1)}, f32[16,8,512]{2,1,0:T(8,128)S(1)}, u32[]{:S(2)}, u32[]{:S(2)}) collective-permute-start(f32[16,8,512]{2,1,0:T(8,128)S(1)} %all-to-all-done.1.mine), channel_id=1, source_target_pairs={{0,4},{4,0},{8,12},{12,8},{1,5},{5,1},{9,13},{13,9},{2,6},{6,2},{1... | collective-permute-start | bytes 786440 | tf_op jit(solution)/shard_map/ppermute | solution.py:353

commit v3 on v2

--- a/solution.py
+++ b/solution.py
@@ -271,7 +271,7 @@
         ]
 
     pairs = (
-        ((0, BATCH, 0), (3, BATCH // 2, BATCH)),
+        ((0, BATCH, 0), (3, 6, BATCH)),
         ((1, 6, 2 * BATCH), (2, 6, 3 * BATCH)),
     )
     for pair in pairs:

time: 26.4 us -> 26.7 us (1.011)
  the two profiles are of different devices: /device:TPU:1 before, /device:TPU:0 now
where the time goes in v3:
time: 26.7 us; the launch traced here: 27.1 us
  waiting for transfers between devices  9.34 us (35%)
  Pallas kernels  8.87 us (33%)
  starting transfers between devices  7.49 us (28%)
  between operations  0.7 us (3%)
  other arithmetic  0.69 us (3%)
    all_to_all x1, waiting for transfers between devices, exchange(): lax.all_to_all(outgoing.reshape(tiles, 8, rays + LANES), ('row', 'col'),...  9.15 us
    all_to_all x1, starting transfers between devices, exchange(): lax.all_to_all(outgoing.reshape(tiles, 8, rays + LANES), ('row', 'col'),...  7.49 us
    pallas_call x1, Pallas kernels, deposit(): pl.pallas_call(kernel, out_shape=(jax.ShapeDtypeStruct((TILE, TILE), jnp....  5.81 us
    pallas_call x1, Pallas kernels, exchange(): pl.pallas_call(kernel, out_shape=jax.ShapeDtypeStruct((8 * tiles, rays +...  2.18 us
    pallas_call x1, Pallas kernels, shards(): pl.pallas_call(table_kernel, out_shape=(jax.ShapeDtypeStruct((TURNS * LAN...  0.88 us
    reduce_max x1, other arithmetic, shards(): turns = jnp.max(mine[:, 7, 2 * LANES + COUNT]).astype(jnp.int32)  0.69 us
  transfers between devices with their start and end apart: 2, of which 2 were waited for; matrix products, arithmetic and copies ran while one was open for 3% of the time, Pallas kernels for 3%

profile of v3, /device:TPU:0, one launch (start us, length us, event | category | flops | bytes accessed | tf_op | source)
XLA Modules:
  0.0 27.1 jit_solution(14782826036788128596)
XLA Ops:
  0.0 2.2 %pack.2 = f32[128,512]{1,0:T(8,128)} custom-call(s32[1,16]{1,0:T(1,128)} %bitcast.9, f32[16,2,384]{2,1,0:T(2,128)} %rays_ref.3), custom_call_target="tpu_custom_call" | custom-call | tf_op jit(solution)/shard_map/pack/pallas_call | solution.py:336
  2.2 0.0 copy-start
  2.2 0.0 copy-start.1
  2.2 0.0 copy-start.2
  2.2 7.5 %all-to-all-start.1 = ((f32[16,8,512]{2,1,0:T(8,128)}), f32[16,8,512]{2,1,0:T(8,128)S(1)}, u32[]{:S(2)}, u32[]{:S(2)}) async-start(f32[16,8,512]{2,1,0:T(8,128)} %bitcast.11), calls=%async_computation.1 | async-start | bytes 524288 | tf_op jit(solution)/shard_map/all_to_all | solution.py:348
  9.7 0.0 copy-done
  9.7 0.0 copy-done.1
  9.7 0.0 copy-done.2
  9.7 0.9 %table.1 = (bf16[512,1024]{1,0:T(8,128)(2,1)S(1)}, bf16[128,128]{1,0:T(8,128)(2,1)S(1)}, s32[1,16]{1,0:T(1,128)S(1)}, f32[16,2,384]{2,1,0:T(2,128)S(1)}) custom-call(f32[65,65]{1,0:T(8,128)S(1)} %copy-done.1, s32[1,16]{1,0:T(1,128)S(1)} %bitcast.10, f32[16,2,384]{2,1,0:T(2,128)S(1)} %copy-done), custom_call_target="tpu_custom_call" | custom-call | flops 10000000 | bytes 6000000 | tf_op jit(solution)/shard_map/table/pallas_call | solution.py:380
  10.6 9.2 %all-to-all-done.1.mine = f32[16,8,512]{2,1,0:T(8,128)S(1)} async-done(((f32[16,8,512]{2,1,0:T(8,128)}), f32[16,8,512]{2,1,0:T(8,128)S(1)}, u32[]{:S(2)}, u32[]{:S(2)}) %all-to-all-start.1) | async-done | bytes 262176 | tf_op jit(solution)/shard_map/all_to_all | solution.py:348
  19.7 0.0 collective-permute-start.1
  19.8 0.7 %slice_reduce_fusion = f32[]{:T(128)} fusion(f32[16,8,512]{2,1,0:T(8,128)S(1)} %all-to-all-done.1.mine), kind=kLoop, calls=%fused_computation | loop fusion | flops 15 | bytes 68 | tf_op jit(solution)/shard_map/reduce_max | solution.py:395
  21.1 0.2 collective-permute-done.1.other
  21.3 5.8 %spread.2 = (f32[128,128]{1,0:T(8,128)}, f32[192,192]{1,0:T(8,128)S(1)}) custom-call(f32[16,8,512]{2,1,0:T(8,128)S(1)} %all-to-all-done.1.mine, f32[16,8,512]{2,1,0:T(8,128)S(1)} %collective-permute-done.1.other, bf16[512,1024]{1,0:T(8,128)(2,1)S(1)} %get-tuple-element.146.refs_0_, bf16[128,128]{1,0:T(8,128)(2,1)S(1)} %get-tuple-element.147.refs_1_), custom_call_target="tpu_custom_call" | custom-call | tf_op jit(solution)/shard_map/spread/pallas_call | solution.py:359
  (1 shorter events, 0.0 us)
Async XLA Ops:
  2.2 7.5 %copy-start = (f32[16,2,384]{2,1,0:T(2,128)S(1)}, f32[16,2,384]{2,1,0:T(2,128)}, u32[]{:S(2)}) copy-start(f32[16,2,384]{2,1,0:T(2,128)} %rays_ref.3) | copy-start | bytes 147460
  2.2 7.5 %copy-start.1 = (f32[65,65]{1,0:T(8,128)S(1)}, f32[65,65]{1,0:T(8,128)}, u32[]{:S(2)}) copy-start(f32[65,65]{1,0:T(8,128)} %profile_ref.1) | copy-start | bytes 50704
  2.2 7.5 %copy-start.2 = (s32[16,1]{0,1:T(1,128)S(1)}, s32[16,1]{0,1:T(1,128)}, u32[]{:S(2)}) copy-start(s32[16,1]{0,1:T(1,128)} %param.6) | copy-start | bytes 196
  2.2 17.6 %all-to-all-start.1 = ((f32[16,8,512]{2,1,0:T(8,128)}), f32[16,8,512]{2,1,0:T(8,128)S(1)}, u32[]{:S(2)}, u32[]{:S(2)}) async-start(f32[16,8,512]{2,1,0:T(8,128)} %bitcast.11), calls=%async_computation.1 | async-start | bytes 524288 | tf_op jit(solution)/shard_map/all_to_all | solution.py:348
  19.7 1.5 %collective-permute-start.1 = (f32[16,8,512]{2,1,0:T(8,128)S(1)}, f32[16,8,512]{2,1,0:T(8,128)S(1)}, u32[]{:S(2)}, u32[]{:S(2)}) collective-permute-start(f32[16,8,512]{2,1,0:T(8,128)S(1)} %all-to-all-done.1.mine), channel_id=1, source_target_pairs={{0,4},{4,0},{8,12},{12,8},{1,5},{5,1},{9,13},{13,9},{2,6},{6,2},{1... | collective-permute-start | bytes 786440 | tf_op jit(solution)/shard_map/ppermute | solution.py:353

commit v4 on v2

--- a/solution.py
+++ b/solution.py
@@ -272,7 +272,7 @@
 
     pairs = (
         ((0, BATCH, 0), (3, BATCH // 2, BATCH)),
-        ((1, 6, 2 * BATCH), (2, 6, 3 * BATCH)),
+        ((1, BATCH, 2 * BATCH), (2, BATCH, 3 * BATCH)),
     )
     for pair in pairs:
         kinds = [kind for kind, _, _ in pair]

time: 26.4 us -> 26.4 us (level); the launches traced: 26.4 us -> 26.1 us
  Pallas kernels: 8.29 us -> 7.98 us
    pallas_call x1, Pallas kernels: 5.23 us -> 4.92 us  [deposit(): pl.pallas_call(kernel, out_shape=(jax.ShapeDtypeStruct((TILE, TILE), jnp....]
where the time goes in v4:
time: 26.4 us; the launch traced here: 26.1 us
  waiting for transfers between devices  8.44 us (32%)
  starting transfers between devices  8.27 us (31%)
  Pallas kernels  7.98 us (30%)
  other arithmetic  0.69 us (3%)
  between operations  0.69 us (3%)
    all_to_all x1, waiting for transfers between devices, exchange(): lax.all_to_all(outgoing.reshape(tiles, 8, rays + LANES), ('row', 'col'),...  8.43 us
    all_to_all x1, starting transfers between devices, exchange(): lax.all_to_all(outgoing.reshape(tiles, 8, rays + LANES), ('row', 'col'),...  7.45 us
    pallas_call x1, Pallas kernels, deposit(): pl.pallas_call(kernel, out_shape=(jax.ShapeDtypeStruct((TILE, TILE), jnp....  4.92 us
    pallas_call x1, Pallas kernels, exchange(): pl.pallas_call(kernel, out_shape=jax.ShapeDtypeStruct((8 * tiles, rays +...  2.18 us
    pallas_call x1, Pallas kernels, shards(): pl.pallas_call(table_kernel, out_shape=(jax.ShapeDtypeStruct((TURNS * LAN...  0.88 us
    ppermute x1, starting transfers between devices, deposit(): other = lax.ppermute(mine, 'row', [(i, i ^ 1) for i in range(row_count)])  0.82 us
    reduce_max x1, other arithmetic, shards(): turns = jnp.max(mine[:, 7, 2 * LANES + COUNT]).astype(jnp.int32)  0.69 us
  transfers between devices with their start and end apart: 2, of which 1 were waited for; matrix products, arithmetic and copies ran while one was open for 3% of the time, Pallas kernels for 3%

profile of v4, /device:TPU:1, one launch (start us, length us, event | category | flops | bytes accessed | tf_op | source)
XLA Modules:
  0.0 26.1 jit_solution(7612107567447813567)
XLA Ops:
  0.0 2.2 %pack.2 = f32[128,512]{1,0:T(8,128)} custom-call(s32[1,16]{1,0:T(1,128)} %bitcast.9, f32[16,2,384]{2,1,0:T(2,128)} %rays_ref.3), custom_call_target="tpu_custom_call" | custom-call | tf_op jit(solution)/shard_map/pack/pallas_call | solution.py:336
  2.2 0.0 copy-start
  2.2 0.0 copy-start.1
  2.2 0.0 copy-start.2
  2.2 7.5 %all-to-all-start.1 = ((f32[16,8,512]{2,1,0:T(8,128)}), f32[16,8,512]{2,1,0:T(8,128)S(1)}, u32[]{:S(2)}, u32[]{:S(2)}) async-start(f32[16,8,512]{2,1,0:T(8,128)} %bitcast.11), calls=%async_computation.1 | async-start | bytes 524288 | tf_op jit(solution)/shard_map/all_to_all | solution.py:348
  9.6 0.0 copy-done
  9.6 0.0 copy-done.1
  9.7 0.0 copy-done.2
  9.7 0.9 %table.1 = (bf16[512,1024]{1,0:T(8,128)(2,1)S(1)}, bf16[128,128]{1,0:T(8,128)(2,1)S(1)}, s32[1,16]{1,0:T(1,128)S(1)}, f32[16,2,384]{2,1,0:T(2,128)S(1)}) custom-call(f32[65,65]{1,0:T(8,128)S(1)} %copy-done.1, s32[1,16]{1,0:T(1,128)S(1)} %bitcast.10, f32[16,2,384]{2,1,0:T(2,128)S(1)} %copy-done), custom_call_target="tpu_custom_call" | custom-call | flops 10000000 | bytes 6000000 | tf_op jit(solution)/shard_map/table/pallas_call | solution.py:380
  10.6 8.4 %all-to-all-done.1.mine = f32[16,8,512]{2,1,0:T(8,128)S(1)} async-done(((f32[16,8,512]{2,1,0:T(8,128)}), f32[16,8,512]{2,1,0:T(8,128)S(1)}, u32[]{:S(2)}, u32[]{:S(2)}) %all-to-all-start.1) | async-done | bytes 262176 | tf_op jit(solution)/shard_map/all_to_all | solution.py:348
  19.0 0.8 %collective-permute-start.1 = (f32[16,8,512]{2,1,0:T(8,128)S(1)}, f32[16,8,512]{2,1,0:T(8,128)S(1)}, u32[]{:S(2)}, u32[]{:S(2)}) collective-permute-start(f32[16,8,512]{2,1,0:T(8,128)S(1)} %all-to-all-done.1.mine), channel_id=1, source_target_pairs={{0,4},{4,0},{8,12},{12,8},{1,5},{5,1},{9,13},{13,9},{2,6},{6,2},{1... | collective-permute-start | bytes 786440 | tf_op jit(solution)/shard_map/ppermute | solution.py:353
  19.8 0.7 %slice_reduce_fusion = f32[]{:T(128)} fusion(f32[16,8,512]{2,1,0:T(8,128)S(1)} %all-to-all-done.1.mine), kind=kLoop, calls=%fused_computation | loop fusion | flops 15 | bytes 68 | tf_op jit(solution)/shard_map/reduce_max | solution.py:395
  21.1 0.0 collective-permute-done.1.other
  21.2 4.9 %spread.2 = (f32[128,128]{1,0:T(8,128)}, f32[192,192]{1,0:T(8,128)S(1)}) custom-call(f32[16,8,512]{2,1,0:T(8,128)S(1)} %all-to-all-done.1.mine, f32[16,8,512]{2,1,0:T(8,128)S(1)} %collective-permute-done.1.other, bf16[512,1024]{1,0:T(8,128)(2,1)S(1)} %get-tuple-element.146.refs_0_, bf16[128,128]{1,0:T(8,128)(2,1)S(1)} %get-tuple-element.147.refs_1_), custom_call_target="tpu_custom_call" | custom-call | tf_op jit(solution)/shard_map/spread/pallas_call | solution.py:359
  (1 shorter events, 0.0 us)
Async XLA Ops:
  2.2 7.5 %copy-start = (f32[16,2,384]{2,1,0:T(2,128)S(1)}, f32[16,2,384]{2,1,0:T(2,128)}, u32[]{:S(2)}) copy-start(f32[16,2,384]{2,1,0:T(2,128)} %rays_ref.3) | copy-start | bytes 147460
  2.2 7.5 %copy-start.1 = (f32[65,65]{1,0:T(8,128)S(1)}, f32[65,65]{1,0:T(8,128)}, u32[]{:S(2)}) copy-start(f32[65,65]{1,0:T(8,128)} %profile_ref.1) | copy-start | bytes 50704
  2.2 7.5 %copy-start.2 = (s32[16,1]{0,1:T(1,128)S(1)}, s32[16,1]{0,1:T(1,128)}, u32[]{:S(2)}) copy-start(s32[16,1]{0,1:T(1,128)} %param.6) | copy-start | bytes 196
  2.2 16.8 %all-to-all-start.1 = ((f32[16,8,512]{2,1,0:T(8,128)}), f32[16,8,512]{2,1,0:T(8,128)S(1)}, u32[]{:S(2)}, u32[]{:S(2)}) async-start(f32[16,8,512]{2,1,0:T(8,128)} %bitcast.11), calls=%async_computation.1 | async-start | bytes 524288 | tf_op jit(solution)/shard_map/all_to_all | solution.py:348
  19.0 2.2 %collective-permute-start.1 = (f32[16,8,512]{2,1,0:T(8,128)S(1)}, f32[16,8,512]{2,1,0:T(8,128)S(1)}, u32[]{:S(2)}, u32[]{:S(2)}) collective-permute-start(f32[16,8,512]{2,1,0:T(8,128)S(1)} %all-to-all-done.1.mine), channel_id=1, source_target_pairs={{0,4},{4,0},{8,12},{12,8},{1,5},{5,1},{9,13},{13,9},{2,6},{6,2},{1... | collective-permute-start | bytes 786440 | tf_op jit(solution)/shard_map/ppermute | solution.py:353
